TPU v7x, 32 devices: a whole 2x2x4 slice. The times are simulated.
32 devices in a mesh: parts: 2 (over x), ref: 16 (over z, y, core).
Axes of the slice: x: 2, y: 2, z: 4, core: 2. Of those that a mesh axis runs over, the one named last changes fastest.
Arguments:
- queries: float32 [4096, 128], P('parts'), parts along dimension 0, may hold values from -15 to 15, as said below
- references: float32 [65536, 128], P(('parts', 'ref')), parts along dimension 0, may hold values from -15 to 15
- query_ids: int32 [4096], P('parts'), parts along dimension 0, may hold values from 0 to 32767, as said below
- spread: float32 [128], replicated, may hold values from 0.5 to 2
- cotangent: float32 [4096], P('parts'), parts along dimension 0, may hold values from -4 to 4
Outputs:
- query_grad: float32 [4096, 128], P(('parts', 'ref')), parts along dimension 0
- reference_grad: float32 [65536, 128], P(('parts', 'ref')), parts along dimension 0
- spread_grad: float32 [256], P('parts'), parts along dimension 0
There are 2 independent parts, one for each index of `parts`. A program takes and returns all parts, laid end to end along the dimension named above; an argument that names none is the same for every part. Nothing has to cross between parts.
Inputs may be any that keep to these rules, and one draw needn't show every extreme that they name: `query_ids`: distinct rows of the references; query i is the reference row query_ids_i. `queries`: row i equals row query_ids_i of references.
All inputs are finite; a program needn't handle non-finite values.
Results may differ from a plain program's by a relative error of at most 0.014.
Values sent between devices are 32-bit elements; how exact they have to be, the bound alone decides.
A program may use at most 64 MiB of HBM per device.

v0:
```python
import jax
import jax.numpy as jnp
from jax import lax
from jax.sharding import PartitionSpec as P


def block_score(query_block, id_block, references, rnorm, inv, ref_start):
    cross = lax.dot_general(
        query_block * inv,
        references,
        (((1,), (1,)), ((), ())),
        precision=lax.Precision.HIGHEST,
        preferred_element_type=jnp.float32,
    )
    qnorm = jnp.sum(query_block * query_block * inv, axis=1)
    score = cross - 0.5 * qnorm[:, None] - 0.5 * rnorm[None, :]
    local_ids = id_block - ref_start
    self_mask = local_ids[:, None] == lax.iota(jnp.int32, references.shape[0])[None, :]
    return (jnp.where(self_mask, -jnp.inf, score), self_mask)


def on_device(queries, references, query_ids, spread, cotangent):
    n_query = queries.shape[0]
    n_feat = queries.shape[1]
    n_ref = references.shape[0]
    block_rows = min(512, n_query)
    n_blocks = n_query // block_rows
    inv = 1.0 / (spread * spread)
    rnorm = jnp.sum(references * references * inv, axis=1)
    ref_start = lax.axis_index("ref") * n_ref
    query_blocks = queries.reshape(n_blocks, block_rows, n_feat)
    id_blocks = query_ids.reshape(n_blocks, block_rows)
    weight_blocks = cotangent.reshape(n_blocks, block_rows)

    def local_density(items):
        query_block, id_block = items
        score, self_mask = block_score(query_block, id_block, references, rnorm, inv, ref_start)
        local_peak = jnp.max(score, axis=1)
        local_total = jnp.sum(jnp.exp(score - local_peak[:, None]), axis=1)
        return (local_peak, local_total)

    local_peak, local_total = lax.map(local_density, (query_blocks, id_blocks))
    local_peak = local_peak.reshape(n_query)
    local_total = local_total.reshape(n_query)
    peak = lax.pmax(local_peak, "ref")
    total = lax.psum(local_total * jnp.exp(local_peak - peak), "ref")
    ref_low = references.astype(jnp.bfloat16)
    query_low_blocks = query_blocks.astype(jnp.bfloat16)

    def backward(carry, items):
        pushed, column = carry
        query_block, query_low, id_block, cot_block, peak_block, total_block = items
        score, self_mask = block_score(query_block, id_block, references, rnorm, inv, ref_start)
        weight = jnp.where(
            self_mask,
            0.0,
            cot_block[:, None] * jnp.exp(score - peak_block[:, None]) / total_block[:, None],
        ).astype(jnp.bfloat16)
        pulled = jnp.dot(weight, ref_low, preferred_element_type=jnp.float32)
        pushed = pushed + lax.dot_general(
            weight, query_low, (((0,), (0,)), ((), ())), preferred_element_type=jnp.float32
        )
        column = column + jnp.sum(weight.astype(jnp.float32), axis=0)
        return ((pushed, column), pulled)

    init = (jnp.zeros((n_ref, n_feat), jnp.float32), jnp.zeros((n_ref,), jnp.float32))
    items = (
        query_blocks,
        query_low_blocks,
        id_blocks,
        weight_blocks,
        peak.reshape(n_blocks, block_rows),
        total.reshape(n_blocks, block_rows),
    )
    (pushed, column), pulled = lax.scan(backward, init, items)
    pulled = pulled.reshape(n_query, n_feat)
    reference_grad = (pushed - references * column[:, None]) * inv
    ref_terms = jnp.sum(references * reference_grad, axis=0)
    weight_total = jnp.sum(cotangent)
    own_rows = n_query // lax.axis_size("ref")
    own_start = lax.axis_index("ref") * own_rows
    summed_pull, summed_terms = lax.psum((pulled, ref_terms), "ref")
    every_grad = (summed_pull - queries * cotangent[:, None]) * inv
    summed = jnp.sum(queries * every_grad, axis=0) + summed_terms
    query_grad = lax.dynamic_slice_in_dim(every_grad, own_start, own_rows, 0)
    spread_grad = -summed / spread - weight_total / spread
    return (query_grad, reference_grad, spread_grad)


def solution(mesh):
    placed = (P("parts", None), P(("parts", "ref"), None), P("parts"), P(), P("parts"))
    return jax.shard_map(
        on_device,
        mesh=mesh,
        in_specs=placed,
        out_specs=(P(("parts", "ref"), None), P(("parts", "ref"), None), P("parts")),
        check_vma=False,
    )
```

profile of v0, /device:TPU:0, one launch (start us, length us, event | category | flops | bytes accessed | tf_op | source)
XLA Modules:
  0.0 282.2 jit_solution(32626793319487471)
XLA Ops:
  7.2 0.0 all-reduce.2.cloned.1.call-start
  7.3 0.7 multiply_divide_fusion
  7.9 0.7 reshape.72
  8.6 0.7 reshape.73
  9.3 1.3 convert_element_type.12
  10.6 1.9 fusion.15
  12.5 30.2 %while.27 = (s32[]{:T(128)}, f32[4,512]{1,0:T(4,128)S(1)}, f32[4,512]{1,0:T(4,128)S(1)}, s32[4,512]{1,0:T(4,128)S(1)}, s32[]{:T(128)}, /*index=5*/f32[4,512,128]...) while((s32[]{:T(128)}, f32[4,512]{1,0:T(4,128)S(1)}, ...), condition=%wide.region_5.6_spmd, body=%wide.region_1.5_spmd.sunk | while | flops 1618216448 | bytes 10015885 | solution.py:42
  12.6 1.1 fusion.32
  13.7 5.6 %fusion.33 = (f32[512]{0:T(512)S(1)}, f32[512,2048]{1,0:T(8,128)S(1)}) fusion(f32[2048]{0:T(1024)S(1)} %broadcast_multiply_fusion.8, f32[512]{0:T(512)S(1)} %broadcast_multiply_fusion.9, f32[2048,128]{1,0:T(8,128)} %get-tuple-element.432, f32[4,512,128]{2,1,0:T(8,128)} %get-tuple-element.430, s32[]{:T(128)S(6)} %copy.16, ...), kind=kOutput, calls=%fused_computation.45.clone.1 | convolution fusion | flops 1615920640 | bytes 5519876 | tf_op jit(solution)/shard_map/while/body/eval_jaxpr/dot_general | solution.py:8
  19.3 0.7 exponential_reduce_fusion.2
  20.0 0.1 dynamic_update_slice.17
  20.1 1.1 fusion.32
  21.2 5.6 %fusion.33 = (f32[512]{0:T(512)S(1)}, f32[512,2048]{1,0:T(8,128)S(1)}) fusion(f32[2048]{0:T(1024)S(1)} %broadcast_multiply_fusion.8, f32[512]{0:T(512)S(1)} %broadcast_multiply_fusion.9, f32[2048,128]{1,0:T(8,128)} %get-tuple-element.432, f32[4,512,128]{2,1,0:T(8,128)} %get-tuple-element.430, s32[]{:T(128)S(6)} %copy.16, ...), kind=kOutput, calls=%fused_computation.45.clone.1 | convolution fusion | flops 1615920640 | bytes 5519876 | tf_op jit(solution)/shard_map/while/body/eval_jaxpr/dot_general | solution.py:8
  26.8 0.7 exponential_reduce_fusion.2
  27.6 0.1 dynamic_update_slice.17
  27.7 1.1 fusion.32
  28.8 5.6 %fusion.33 = (f32[512]{0:T(512)S(1)}, f32[512,2048]{1,0:T(8,128)S(1)}) fusion(f32[2048]{0:T(1024)S(1)} %broadcast_multiply_fusion.8, f32[512]{0:T(512)S(1)} %broadcast_multiply_fusion.9, f32[2048,128]{1,0:T(8,128)} %get-tuple-element.432, f32[4,512,128]{2,1,0:T(8,128)} %get-tuple-element.430, s32[]{:T(128)S(6)} %copy.16, ...), kind=kOutput, calls=%fused_computation.45.clone.1 | convolution fusion | flops 1615920640 | bytes 5519876 | tf_op jit(solution)/shard_map/while/body/eval_jaxpr/dot_general | solution.py:8
  34.4 0.7 exponential_reduce_fusion.2
  35.1 0.1 dynamic_update_slice.17
  35.2 1.1 fusion.32
  36.3 5.6 %fusion.33 = (f32[512]{0:T(512)S(1)}, f32[512,2048]{1,0:T(8,128)S(1)}) fusion(f32[2048]{0:T(1024)S(1)} %broadcast_multiply_fusion.8, f32[512]{0:T(512)S(1)} %broadcast_multiply_fusion.9, f32[2048,128]{1,0:T(8,128)} %get-tuple-element.432, f32[4,512,128]{2,1,0:T(8,128)} %get-tuple-element.430, s32[]{:T(128)S(6)} %copy.16, ...), kind=kOutput, calls=%fused_computation.45.clone.1 | convolution fusion | flops 1615920640 | bytes 5519876 | tf_op jit(solution)/shard_map/while/body/eval_jaxpr/dot_general | solution.py:8
  41.9 0.7 exponential_reduce_fusion.2
  42.7 0.1 dynamic_update_slice.17
  42.8 35.4 %pmax.7 = f32[2048]{0:T(1024)S(1)} all-reduce(f32[2048]{0:T(1024)S(1)} %bitcast.87), channel_id=1, replica_groups=mesh['parts'=2,'ref'=16] {'ref'}, use_global_device_ids=true, to_apply=%region_6.7 | all-reduce | flops 2048 | bytes 16384 | tf_op jit(solution)/shard_map/pmax | solution.py:45
  78.2 30.2 %psum.21 = f32[4,512]{1,0:T(4,128)S(1)} all-reduce(f32[4,512]{1,0:T(4,128)S(1)} %reshape.78), channel_id=1, replica_groups=mesh['parts'=2,'ref'=16] {'ref'}, use_global_device_ids=true, to_apply=%region_7.8 | all-reduce | flops 2048 | bytes 16384 | tf_op jit(solution)/shard_map/psum | solution.py:46
  108.4 0.0 copy-start
  108.4 40.8 %while.28 = (s32[]{:T(128)}, f32[2048,128]{1,0:T(8,128)S(1)}, f32[2048]{0:T(1024)S(1)}, f32[4,512,128]{2,1,0:T(8,128)}, s32[4,512]{1,0:T(4,128)S(1)}, /*index=5*...) while((s32[]{:T(128)}, f32[2048,128]{1,0:T(8,128)S(1)}, ...), condition=%wide.region_11.12_spmd.clone, body=%wide.region_8.11_spmd.clone.sunk | while | flops 2159809024 | bytes 10970320 | solution.py:75
  108.5 1.1 fusion.39
  109.6 6.4 %convert_reduce_fusion.2 = (f32[2048]{0:T(1024)S(1)}, bf16[512,2048]{1,0:T(8,128)(2,1)S(1)}) fusion(f32[512]{0:T(512)S(1)} %bitcast.89, f32[512]{0:T(512)S(1)} %bitcast.90, f32[2048]{0:T(1024)S(1)} %broadcast_multiply_fusion.10, f32[512]{0:T(512)S(1)} %broadcast_multiply_fusion.11, f32[2048,128]{1,0:T(8,128)} %get-tuple-element.479, ...), kind=kOutput, calls=%fused_computation.13.clone.1 | convolution fusion | flops 1622210560 | bytes 3435012 | tf_op jit(solution)/shard_map/while/body/eval_jaxpr/dot_general | solution.py:8
  116.1 1.2 convolution_add_fusion.2
  117.3 1.4 fusion.40
  118.7 1.1 fusion.39
  119.8 6.4 %convert_reduce_fusion.2 = (f32[2048]{0:T(1024)S(1)}, bf16[512,2048]{1,0:T(8,128)(2,1)S(1)}) fusion(f32[512]{0:T(512)S(1)} %bitcast.89, f32[512]{0:T(512)S(1)} %bitcast.90, f32[2048]{0:T(1024)S(1)} %broadcast_multiply_fusion.10, f32[512]{0:T(512)S(1)} %broadcast_multiply_fusion.11, f32[2048,128]{1,0:T(8,128)} %get-tuple-element.479, ...), kind=kOutput, calls=%fused_computation.13.clone.1 | convolution fusion | flops 1622210560 | bytes 3435012 | tf_op jit(solution)/shard_map/while/body/eval_jaxpr/dot_general | solution.py:8
  126.3 1.2 convolution_add_fusion.2
  127.5 1.4 fusion.40
  128.9 1.1 fusion.39
  130.0 6.4 %convert_reduce_fusion.2 = (f32[2048]{0:T(1024)S(1)}, bf16[512,2048]{1,0:T(8,128)(2,1)S(1)}) fusion(f32[512]{0:T(512)S(1)} %bitcast.89, f32[512]{0:T(512)S(1)} %bitcast.90, f32[2048]{0:T(1024)S(1)} %broadcast_multiply_fusion.10, f32[512]{0:T(512)S(1)} %broadcast_multiply_fusion.11, f32[2048,128]{1,0:T(8,128)} %get-tuple-element.479, ...), kind=kOutput, calls=%fused_computation.13.clone.1 | convolution fusion | flops 1622210560 | bytes 3435012 | tf_op jit(solution)/shard_map/while/body/eval_jaxpr/dot_general | solution.py:8
  136.5 1.2 convolution_add_fusion.2
  137.7 1.4 fusion.40
  139.1 1.1 fusion.39
  140.2 6.4 %convert_reduce_fusion.2 = (f32[2048]{0:T(1024)S(1)}, bf16[512,2048]{1,0:T(8,128)(2,1)S(1)}) fusion(f32[512]{0:T(512)S(1)} %bitcast.89, f32[512]{0:T(512)S(1)} %bitcast.90, f32[2048]{0:T(1024)S(1)} %broadcast_multiply_fusion.10, f32[512]{0:T(512)S(1)} %broadcast_multiply_fusion.11, f32[2048,128]{1,0:T(8,128)} %get-tuple-element.479, ...), kind=kOutput, calls=%fused_computation.13.clone.1 | convolution fusion | flops 1622210560 | bytes 3435012 | tf_op jit(solution)/shard_map/while/body/eval_jaxpr/dot_general | solution.py:8
  146.7 1.2 convolution_add_fusion.2
  147.8 1.4 fusion.40
  149.3 0.0 copy-start.1
  149.3 0.0 all-reduce.2.cloned.1.call-update
  149.3 0.0 copy-done
  149.3 0.7 reduce_sum.75
  150.0 89.9 %all-reduce.2.cloned.1.call-done = f32[2048,128]{1,0:T(8,128)} async-done(((f32[2048,128]{1,0:T(8,128)}), f32[2048,128]{1,0:T(8,128)}) %all-reduce.2.cloned.1.call-update) | async-done | bytes 1048592 | tf_op jit(solution)/shard_map/psum | solution.py:82
  239.9 3.0 %multiply_reduce_fusion = (f32[128]{0:T(128)S(1)}, f32[2048,128]{1,0:T(8,128)}, f32[128]{0:T(128)S(1)}, f32[2048,128]{1,0:T(8,128)S(1)}) fusion(f32[2048,128]{1,0:T(8,128)} %get-tuple-element.491, f32[128]{0:T(128)S(1)} %get-tuple-element.498, f32[2048,128]{1,0:T(8,128)S(1)} %get-tuple-element.133, f32[2048]{0:T(1024)S(1)} %get-tuple-element.134, ...), kind=kLoop, calls=%fused_computation.36 | loop fusion | flops 2621184 | bytes 6309376 | tf_op jit(solution)/shard_map/reduce_sum | solution.py:78
  242.9 30.6 %psum.23 = f32[128]{0:T(128)S(1)} all-reduce(f32[128]{0:T(128)S(1)} %get-tuple-element.231), channel_id=1, replica_groups=mesh['parts'=2,'ref'=16] {'ref'}, use_global_device_ids=true, to_apply=%region_15.16 | all-reduce | flops 128 | bytes 1024 | tf_op jit(solution)/shard_map/psum | solution.py:82
  273.5 0.6 constant_dynamic-slice_fusion.3
  274.1 0.0 copy-done.1
  274.1 1.2 divide_subtract_fusion
  (50 shorter events, 0.5 us)
Async XLA Ops:
  7.2 232.7 %all-reduce.2.cloned.1.call-start = ((), (), s32[]{:S(2)}) async-start(), calls=%async_computation | async-start | bytes 2097152 | tf_op jit(solution)/shard_map/psum | solution.py:82
  108.4 40.9 %copy-start = (f32[2048]{0:T(1024)S(1)}, f32[2048]{0:T(1024)}, u32[]{:S(2)}) copy-start(f32[2048]{0:T(1024)} %param.13) | copy-start | bytes 24580
  149.3 124.8 %copy-start.1 = (f32[128]{0:T(128)S(1)}, f32[128]{0:T(128)}, u32[]{:S(2)}) copy-start(f32[128]{0:T(128)} %param.12) | copy-start | bytes 1540
Sparse Core Ops, SparseCore 0:
  149.4 90.4 all-reduce.1
where the time goes:
time: 283 us; the launch traced here: 282 us
  blocking collectives  96.2 us (34%)
  waiting for transfers between devices  89.9 us (32%)
  matrix products  58.3 us (21%)
  other arithmetic  20.5 us (7%)
  between operations  14.2 us (5%)
    psum x1, waiting for transfers between devices, on_device(): summed_pull, summed_terms = lax.psum((pulled, ref_terms), 'ref')  89.9 us
    dot_general x8, matrix products, block_score(): lax.dot_general(query_block * inv, references, (((1,), (1,)), ((), ())),...  47.9 us
    pmax x1, blocking collectives, on_device(): peak = lax.pmax(local_peak, 'ref')  35.4 us
    psum x1, blocking collectives, on_device(): summed_pull, summed_terms = lax.psum((pulled, ref_terms), 'ref')  30.6 us
    psum x1, blocking collectives, on_device(): total = lax.psum(local_total * jnp.exp(local_peak - peak), 'ref')  30.2 us
    reduce_sum x8, other arithmetic, block_score(): qnorm = jnp.sum(query_block * query_block * inv, axis=1)  8.81 us
    dot_general x4, matrix products, backward(): pulled = jnp.dot(weight, ref_low, preferred_element_type=jnp.float32)  5.69 us
  transfers between devices with their start and end apart: 1, of which 1 were waited for; matrix products, arithmetic and copies ran while one was open for 0% of the time, Pallas kernels for 0%

commit v1 on v0

v1 whole, which is shorter than its diff:
```python
import functools
import math

import jax
import jax.numpy as jnp
from jax import lax
from jax.experimental import pallas as pl
from jax.experimental.pallas import tpu as pltpu
from jax.sharding import PartitionSpec as P

LOG2E = math.log2(math.e)
TILE = 256
CHUNK = 512


def split3(x):
    a = x.astype(jnp.bfloat16).astype(jnp.float32)
    b = (x - a).astype(jnp.bfloat16).astype(jnp.float32)
    c = (x - a - b).astype(jnp.bfloat16).astype(jnp.float32)
    return a, b, c


def kernel(
    n, q_ref, r_ref, ids_ref, sp_ref, cot_ref, qg_ref, rg_ref, sg_ref,
    qat, ra, rta, pt, s0, s1, m_ref, ut, cq, qt, xt, lse, lse_rx, term, term_rx, *rest
):
    steps = n.bit_length() - 1
    acc = rest[:steps]
    got = rest[steps:2 * steps]
    ls_send, ls_recv, tm_send, tm_recv, rs_send, rs_recv = rest[2 * steps:]
    nq, nf = q_ref.shape
    nr = r_ref.shape[0]
    own = nq // n
    f32, bf16 = jnp.float32, jnp.bfloat16
    me = lax.axis_index("ref")

    def peer_of(k):
        return lax.rem(me + k, n)

    barrier = pltpu.get_barrier_semaphore()

    def greet(k, carry):
        pl.semaphore_signal(
            barrier, inc=1, device_id={"ref": peer_of(k)}, device_id_type=pl.DeviceIdType.MESH
        )
        return carry

    lax.fori_loop(1, n, greet, 0)

    sp = sp_ref[...]
    inv = 1.0 / (sp * sp)
    inv_col = jnp.transpose(jnp.broadcast_to(inv, (8, nf)))[:, :1]
    for a in range(0, nq, TILE):
        rows = slice(a, a + TILE)
        q_t = jnp.transpose(q_ref[rows, :])
        qt[:, rows] = q_t
        scaled = q_t * (inv_col * LOG2E)
        high = scaled.astype(bf16)
        low = (scaled - high.astype(f32)).astype(bf16)
        qat[0:nf, rows] = high
        qat[nf:2 * nf, rows] = low
        qat[2 * nf:3 * nf, rows] = high
        norm = -0.5 * jnp.sum(q_t * scaled, axis=0, keepdims=True)
        n1, n2, n3 = split3(norm)
        place = lax.broadcasted_iota(jnp.int32, (nf, TILE), 0)
        ext = jnp.where(place < 6, 1.0, 0.0)
        ext = jnp.where(place == 0, n1, ext)
        ext = jnp.where(place == 1, n2, ext)
        ext = jnp.where(place == 2, n3, ext)
        qat[3 * nf:4 * nf, rows] = ext.astype(bf16)
    for a in range(0, nr, TILE):
        rows = slice(a, a + TILE)
        r = r_ref[rows, :]
        high = r.astype(bf16)
        low = (r - high.astype(f32)).astype(bf16)
        ra[rows, 0:nf] = high
        ra[rows, nf:2 * nf] = high
        ra[rows, 2 * nf:3 * nf] = low
        norm = -0.5 * LOG2E * jnp.sum(r * r * inv, axis=1, keepdims=True)
        n1, n2, n3 = split3(norm)
        place = lax.broadcasted_iota(jnp.int32, (TILE, nf), 1)
        ext = jnp.where(place < 6, 1.0, 0.0)
        ext = jnp.where(place == 3, n1, ext)
        ext = jnp.where(place == 4, n2, ext)
        ext = jnp.where(place == 5, n3, ext)
        ra[rows, 3 * nf:4 * nf] = ext.astype(bf16)
        rta[0:nf, rows] = jnp.transpose(r).astype(bf16)
    rta[nf:nf + 16, :] = jnp.ones((16, nr), bf16)

    start = me * nr

    def at(t):
        return pl.ds(pl.multiple_of(t * TILE, TILE), TILE)

    def score(t, s_ref, a, best):
        s = jnp.dot(ra[a:a + CHUNK, :], qat[:, at(t)], preferred_element_type=f32)
        local = ids_ref[:, at(t)] - (start + a)
        hit = lax.broadcasted_iota(jnp.int32, (CHUNK, TILE), 0) == local
        s = jnp.where(hit, -jnp.inf, s)
        s_ref[a:a + CHUNK, :] = s
        top = jnp.max(s, axis=0, keepdims=True)
        return top if best is None else jnp.maximum(best, top)

    def weigh(t, s_ref, a, peak, total):
        p = jnp.exp2(s_ref[a:a + CHUNK, :] - peak).astype(bf16)
        pt[a:a + CHUNK, at(t)] = p
        part = jnp.dot(rta[:, a:a + CHUNK], p, preferred_element_type=f32)
        return part if total is None else total + part

    def stage(ahead, s_ahead, t, s_now):
        best, total = None, None
        peak = None if t is None else m_ref[:, at(t)]
        for a in range(0, nr, CHUNK):
            if ahead is not None:
                best = score(ahead, s_ahead, a, best)
            if t is not None:
                total = weigh(t, s_now, a, peak, total)
        if ahead is not None:
            m_ref[:, at(ahead)] = best
        if t is not None:
            ut[:, at(t)] = total

    tiles = nq // TILE
    stage(0, s0, None, None)

    def pair(t, carry):
        stage(2 * t + 1, s1, 2 * t, s0)
        stage(2 * t + 2, s0, 2 * t + 1, s1)
        return carry

    lax.fori_loop(0, tiles // 2 - 1, pair, 0)
    stage(tiles - 1, s1, tiles - 2, s0)
    stage(None, None, tiles - 1, s1)

    peak = m_ref[...]
    mine = peak + jnp.log(ut[nf:nf + 1, :]) * LOG2E
    lse[...] = mine
    pl.semaphore_wait(barrier, n - 1)

    def all_to(src, dst, send, recv):
        def copy(k):
            return pltpu.make_async_remote_copy(
                src_ref=src, dst_ref=dst.at[k - 1], send_sem=send.at[k - 1], recv_sem=recv.at[k - 1],
                device_id={"ref": peer_of(k)}, device_id_type=pl.DeviceIdType.MESH,
            )

        def begin(k, carry):
            copy(k).start()
            return carry

        def end(k, carry):
            copy(k).wait()
            return carry

        return (lambda: lax.fori_loop(1, n, begin, 0)), (lambda: lax.fori_loop(1, n, end, 0))

    lse_start, lse_wait = all_to(lse, lse_rx, ls_send, ls_recv)
    lse_start()
    cot = cot_ref[...]
    cot_q = jnp.zeros((1, nf), f32)
    for a in range(0, nq, TILE):
        rows = slice(a, a + TILE)
        part = jnp.transpose(qt[:, rows] * cot[:, rows])
        cq[rows, :] = part
        cot_q = cot_q + jnp.sum(part * q_ref[rows, :], axis=0, keepdims=True)
    lse_wait()
    every = lse_rx[...]
    top = jnp.maximum(mine, jnp.max(every, axis=0))
    whole = jnp.exp2(mine - top) + jnp.sum(jnp.exp2(every - top[None]), axis=0)
    coef = cot * jnp.exp2(peak - top) / whole

    terms = jnp.zeros((1, nf), f32)
    for a in range(0, nq, TILE):
        rows = slice(a, a + TILE)
        part = jnp.transpose(ut[0:nf, rows] * coef[:, rows])
        terms = terms + jnp.sum(part * q_ref[rows, :], axis=0, keepdims=True)
        if own >= TILE:
            acc[0][a // (2 * own), (a // own) % 2, a % own:a % own + TILE, :] = part
        else:
            for b in range(0, TILE, own):
                k = (a + b) // own
                acc[0][k // 2, k % 2] = part[b:b + own]

    def halving(b):
        size = 2 ** b
        bit = lax.rem(me // size, 2)
        partner = me + (1 - 2 * bit) * size
        return bit, pltpu.make_async_remote_copy(
            src_ref=acc[b].at[:, 1 - bit], dst_ref=got[b], send_sem=rs_send.at[b], recv_sem=rs_recv.at[b],
            device_id={"ref": partner}, device_id_type=pl.DeviceIdType.MESH,
        )

    def settle(b):
        bit, copy = halving(b)
        copy.wait()
        kept = n // 2 ** (b + 1)
        if b + 1 < steps:
            for k in range(kept):
                acc[b + 1][k // 2, k % 2] = acc[b][k, bit] + got[b][k]
            halving(b + 1)[1].start()
            return None
        return acc[b][0, bit] + got[b][0]

    halving(0)[1].start()

    row = lax.broadcasted_iota(jnp.int32, (nf, TILE), 0)
    for a in range(0, nq, TILE):
        rows = slice(a, a + TILE)
        c = coef[:, rows]
        c1, c2, _ = split3(c)
        extra = jnp.where(row == 0, c1, jnp.where(row == 1, c2, 0.0))
        xt[rows, 0:nf] = jnp.transpose(qt[:, rows] * c).astype(bf16)
        xt[rows, nf:2 * nf] = jnp.transpose(extra).astype(bf16)
    terms = terms * inv
    done = 0
    pulled = None
    chunks = nr // CHUNK
    for i in range(chunks):
        rows = slice(i * CHUNK, (i + 1) * CHUNK)
        both = jnp.dot(pt[rows, :], xt[...], preferred_element_type=f32)
        r = r_ref[rows, :]
        column = both[:, nf:nf + 1] + both[:, nf + 1:nf + 2]
        grad = (both[:, 0:nf] - r * column) * inv
        rg_ref[rows, :] = grad
        terms = terms + jnp.sum(r * grad, axis=0, keepdims=True)
        if i == 0:
            settle(0)
            done = 1
    term[...] = terms
    term_start, term_wait = all_to(term, term_rx, tm_send, tm_recv)
    term_start()
    for b in range(done, steps):
        pulled = settle(b)
    mine_rows = pl.ds(pl.multiple_of(me * own, own), own)
    qg_ref[...] = (pulled - cq[mine_rows, :]) * inv
    term_wait()
    summed = terms + jnp.sum(term_rx[...], axis=0) - cot_q * inv
    sg_ref[...] = -summed / sp - jnp.sum(cot, axis=1, keepdims=True) / sp


def on_device(n, queries, references, query_ids, spread, cotangent):
    nq, nf = queries.shape
    nr = references.shape[0]
    own = nq // n
    steps = n.bit_length() - 1
    f32, bf16 = jnp.float32, jnp.bfloat16
    halves = [n // 2 ** (b + 1) for b in range(steps)]
    scratch = [
        pltpu.VMEM((4 * nf, nq), bf16),
        pltpu.VMEM((nr, 4 * nf), bf16),
        pltpu.VMEM((nf + 16, nr), bf16),
        pltpu.VMEM((nr, nq), bf16),
        pltpu.VMEM((nr, TILE), f32),
        pltpu.VMEM((nr, TILE), f32),
        pltpu.VMEM((1, nq), f32),
        pltpu.VMEM((nf + 16, nq), f32),
        pltpu.VMEM((nq, nf), f32),
        pltpu.VMEM((nf, nq), f32),
        pltpu.VMEM((nq, 2 * nf), bf16),
        pltpu.VMEM((1, nq), f32),
        pltpu.VMEM((n - 1, 1, nq), f32),
        pltpu.VMEM((1, nf), f32),
        pltpu.VMEM((n - 1, 1, nf), f32),
    ]
    scratch += [pltpu.VMEM((h, 2, own, nf), f32) for h in halves]
    scratch += [pltpu.VMEM((h, own, nf), f32) for h in halves]
    scratch += [pltpu.SemaphoreType.DMA((n - 1,))] * 4
    scratch += [pltpu.SemaphoreType.DMA((steps,))] * 2
    vmem = pl.BlockSpec(memory_space=pltpu.VMEM)
    query_grad, reference_grad, spread_grad = pl.pallas_call(
        functools.partial(kernel, n),
        out_shape=(
            jax.ShapeDtypeStruct((own, nf), f32),
            jax.ShapeDtypeStruct((nr, nf), f32),
            jax.ShapeDtypeStruct((1, nf), f32),
        ),
        in_specs=[vmem] * 5,
        out_specs=(vmem, vmem, vmem),
        scratch_shapes=scratch,
        compiler_params=pltpu.CompilerParams(
            collective_id=0, has_side_effects=True, vmem_limit_bytes=52 * 2 ** 20
        ),
    )(queries, references, query_ids[None, :], spread[None, :], cotangent[None, :])
    return query_grad, reference_grad, spread_grad[0]


def solution(mesh):
    placed = (P("parts", None), P(("parts", "ref"), None), P("parts"), P(), P("parts"))
    return jax.shard_map(
        functools.partial(on_device, mesh.shape["ref"]),
        mesh=mesh,
        in_specs=placed,
        out_specs=(P(("parts", "ref"), None), P(("parts", "ref"), None), P("parts")),
        check_vma=False,
    )
```

time: 283 us -> 42.1 us (0.15)
  blocking collectives: 96.2 us -> 0 us
  waiting for transfers between devices: 89.9 us -> 0 us
  matrix products: 58.3 us -> 0 us
  Pallas kernels: 0 us -> 37 us
  other arithmetic: 20.5 us -> 0 us
  between operations: 14.2 us -> 0.65 us
    psum x1 -> x0, waiting for transfers between devices: 89.9 us -> none  [on_device(): summed_pull, summed_terms = lax.psum((pulled, ref_terms), 'ref')]
    psum x2 -> x0, blocking collectives: 60.8 us -> none  [the longest x1 30.6 us: on_device(): summed_pull, summed_terms = lax.psum((pulled, ref_terms), 'ref')]
    dot_general x16 -> x0, matrix products: 58.3 us -> none  [the longest x8 47.9 us: block_score(): lax.dot_general(query_block * inv, references, (((1,), (1,)), ((), ())),...]
    pallas_call x0 -> x1, Pallas kernels: none -> 37 us  [on_device(): pl.pallas_call(functools.partial(kernel, n), out_shape=(jax.ShapeDtypeStr...]
    pmax x1 -> x0, blocking collectives: 35.4 us -> none  [on_device(): peak = lax.pmax(local_peak, 'ref')]
    reduce_sum x14 -> x0, other arithmetic: 15.3 us -> none  [the longest x8 8.81 us: block_score(): qnorm = jnp.sum(query_block * query_block * inv, axis=1)]
    unnamed x6 -> x9, local copies, waits for them, and re-layouts: 0.02 us -> 4.15 us
    convert_element_type x2 -> x0, other arithmetic: 3.18 us -> none  [the longest x1 1.89 us: on_device(): ref_low = references.astype(jnp.bfloat16)]
  transfers between devices with their start and end apart: 1 -> 0, of which waited for: 1 -> 0; matrix products, arithmetic and copies ran while one was open for 0% -> 0% of each run, Pallas kernels for 0% -> 0%
where the time goes in v1:
time: 42.1 us; the launch traced here: 41.8 us
  Pallas kernels  37 us (88%)
  local copies, waits for them, and re-layouts  4.15 us (10%)
  between operations  0.65 us (2%)
    pallas_call x1, Pallas kernels, on_device(): pl.pallas_call(functools.partial(kernel, n), out_shape=(jax.ShapeDtypeStr...  37 us
    unnamed x9, local copies, waits for them, and re-layouts  4.15 us

profile of v1, /device:TPU:0, one launch (start us, length us, event | category | flops | bytes accessed | tf_op | source)
XLA Modules:
  0.0 41.8 jit_solution(13647742983904069688)
XLA Ops:
  0.6 0.0 copy-start.2
  0.6 0.6 %copy-done.2 = f32[128]{0:T(128)S(1)} copy-done((f32[128]{0:T(128)S(1)}, f32[128]{0:T(128)}, u32[]{:S(2)}) %copy-start.2) | copy-done | bytes 536
  1.3 0.0 copy-start
  1.3 0.7 %copy-done = s32[2048]{0:T(1024)S(1)} copy-done((s32[2048]{0:T(1024)S(1)}, s32[2048]{0:T(1024)}, u32[]{:S(2)}) %copy-start) | copy-done | bytes 8216
  2.0 0.0 copy-start.1
  2.0 0.7 %copy-done.1 = f32[2048]{0:T(1024)S(1)} copy-done((f32[2048]{0:T(1024)S(1)}, f32[2048]{0:T(1024)}, u32[]{:S(2)}) %copy-start.1) | copy-done | bytes 8216
  2.7 37.0 %shard_map.76 = (f32[128,128]{1,0:T(8,128)S(1)}, f32[2048,128]{1,0:T(8,128)S(1)}, f32[1,128]{1,0:T(1,128)S(1)}) custom-call(f32[2048,128]{1,0:T(8,128)} %q_ref.1, f32[2048,128]{1,0:T(8,128)} %r_ref.1, s32[1,2048]{1,0:T(1,128)S(1)} %bitcast.4, f32[1,128]{1,0:T(1,128)S(1)} %bitcast.6, f32[1,2048]{1,0:T(1,128)S(1)} %bitcast.5), custom_call_target="tpu_custom_call" | custom-call | tf_op jit(solution)/shard_map/pallas_call | solution.py:270
  39.7 0.6 %copy.11 = f32[128,128]{1,0:T(8,128)} copy(f32[128,128]{1,0:T(8,128)S(1)} %get-tuple-element.12) | data formatting | bytes 131072
  40.3 1.0 %copy.12 = f32[2048,128]{1,0:T(8,128)} copy(f32[2048,128]{1,0:T(8,128)S(1)} %get-tuple-element.13) | data formatting | bytes 2097152
  41.3 0.5 %copy.13 = f32[128]{0:T(128)} copy(f32[128]{0:T(128)S(1)} %bitcast.7) | data formatting | bytes 1024
Async XLA Ops:
  0.6 0.7 %copy-start.2 = (f32[128]{0:T(128)S(1)}, f32[128]{0:T(128)}, u32[]{:S(2)}) copy-start(f32[128]{0:T(128)} %param.8) | copy-start | bytes 1540
  1.3 0.7 %copy-start = (s32[2048]{0:T(1024)S(1)}, s32[2048]{0:T(1024)}, u32[]{:S(2)}) copy-start(s32[2048]{0:T(1024)} %param.7) | copy-start | bytes 24580
  2.0 0.7 %copy-start.1 = (f32[2048]{0:T(1024)S(1)}, f32[2048]{0:T(1024)}, u32[]{:S(2)}) copy-start(f32[2048]{0:T(1024)} %param.9) | copy-start | bytes 24580

commit v2 on v1

v2 whole, which is shorter than its diff:
```python
import functools
import math

import jax
import jax.numpy as jnp
from jax import lax
from jax.experimental import pallas as pl
from jax.experimental.pallas import tpu as pltpu
from jax.sharding import PartitionSpec as P

LOG2E = math.log2(math.e)
TILE = 256
CHUNK = 512


def split3(x):
    a = x.astype(jnp.bfloat16).astype(jnp.float32)
    b = (x - a).astype(jnp.bfloat16).astype(jnp.float32)
    c = (x - a - b).astype(jnp.bfloat16).astype(jnp.float32)
    return a, b, c


def plan(n):
    last = n.bit_length() - 2
    mid = (last + 1) // 2
    first = list(range(last))
    second = [0] + [b for b in range(mid, last)] + [b for b in range(1, mid)]
    return last, (first, second)


def layouts(n):
    last, orders = plan(n)
    shapes = []
    for order in orders:
        left = list(range(last))
        group = []
        for b in order:
            place = left.index(b)
            group.append((2 ** (len(left) - 1 - place), 2, 2 ** place))
            left.remove(b)
        shapes.append(group)
    return shapes


def kernel(
    n, q_ref, r_ref, ids_hbm, sp_hbm, cot_hbm, qg_ref, rg_hbm, sg_ref,
    rg_ref, rg_sem, ids_ref, sp_ref, cot_ref, in_sem,
    qat, ra, rta, pt, s0, s1, m_ref, ut, cq, qt, xt, push, fin, fin_got, term, term_rx, *rest
):
    last, orders = plan(n)
    shapes = layouts(n)
    rest = list(rest)
    lse = [rest.pop(0) for _ in range(2)]
    lse_rx = [rest.pop(0) for _ in range(2)]
    acc = [[rest.pop(0) for _ in range(last)] for _ in range(2)]
    got = [[rest.pop(0) for _ in range(last)] for _ in range(2)]
    ls_send, ls_recv = rest[0:2], rest[2:4]
    rs_send, rs_recv = rest[4:6], rest[6:8]
    tm_send, tm_recv, fin_sem = rest[8:]
    nq, nf = q_ref.shape
    nr = r_ref.shape[0]
    own = nq // n
    half = nq // 2
    f32, bf16 = jnp.float32, jnp.bfloat16
    me = lax.axis_index("ref")

    loads = [
        pltpu.make_async_copy(src, dst, in_sem.at[i])
        for i, (src, dst) in enumerate(((ids_hbm, ids_ref), (sp_hbm, sp_ref), (cot_hbm, cot_ref)))
    ]
    for load in loads:
        load.start()

    def peer_of(k):
        return lax.rem(me + k, n)

    barrier = pltpu.get_barrier_semaphore()

    def greet(k, carry):
        pl.semaphore_signal(
            barrier, inc=1, device_id={"ref": peer_of(k)}, device_id_type=pl.DeviceIdType.MESH
        )
        return carry

    lax.fori_loop(1, n, greet, 0)
    for load in loads:
        load.wait()

    sp = sp_ref[...]
    inv = 1.0 / (sp * sp)
    inv_col = jnp.transpose(jnp.broadcast_to(inv, (8, nf)))[:, :1]
    for a in range(0, nq, TILE):
        rows = slice(a, a + TILE)
        q_t = jnp.transpose(q_ref[rows, :])
        qt[:, rows] = q_t
        scaled = q_t * (inv_col * LOG2E)
        high = scaled.astype(bf16)
        low = (scaled - high.astype(f32)).astype(bf16)
        qat[0:nf, rows] = high
        qat[nf:2 * nf, rows] = low
        qat[2 * nf:3 * nf, rows] = high
        norm = -0.5 * jnp.sum(q_t * scaled, axis=0, keepdims=True)
        n1, n2, n3 = split3(norm)
        place = lax.broadcasted_iota(jnp.int32, (nf, TILE), 0)
        ext = jnp.where(place < 6, 1.0, 0.0)
        ext = jnp.where(place == 0, n1, ext)
        ext = jnp.where(place == 1, n2, ext)
        ext = jnp.where(place == 2, n3, ext)
        qat[3 * nf:4 * nf, rows] = ext.astype(bf16)
    for a in range(0, nr, TILE):
        rows = slice(a, a + TILE)
        r = r_ref[rows, :]
        high = r.astype(bf16)
        low = (r - high.astype(f32)).astype(bf16)
        ra[rows, 0:nf] = high
        ra[rows, nf:2 * nf] = high
        ra[rows, 2 * nf:3 * nf] = low
        norm = -0.5 * LOG2E * jnp.sum(r * r * inv, axis=1, keepdims=True)
        n1, n2, n3 = split3(norm)
        place = lax.broadcasted_iota(jnp.int32, (TILE, nf), 1)
        ext = jnp.where(place < 6, 1.0, 0.0)
        ext = jnp.where(place == 3, n1, ext)
        ext = jnp.where(place == 4, n2, ext)
        ext = jnp.where(place == 5, n3, ext)
        ra[rows, 3 * nf:4 * nf] = ext.astype(bf16)
        rta[0:nf, rows] = jnp.transpose(r).astype(bf16)
    rta[nf:nf + 16, :] = jnp.ones((16, nr), bf16)

    start = me * nr

    def at(t):
        return pl.ds(pl.multiple_of(t * TILE, TILE), TILE)

    def score(t, s_ref, a, best):
        s = jnp.dot(ra[a:a + CHUNK, :], qat[:, at(t)], preferred_element_type=f32)
        local = ids_ref[:, at(t)] - (start + a)
        hit = lax.broadcasted_iota(jnp.int32, (CHUNK, TILE), 0) == local
        s = jnp.where(hit, -jnp.inf, s)
        s_ref[a:a + CHUNK, :] = s
        top = jnp.max(s, axis=0, keepdims=True)
        return top if best is None else jnp.maximum(best, top)

    def weigh(t, s_ref, a, peak, total):
        p = jnp.exp2(s_ref[a:a + CHUNK, :] - peak).astype(bf16)
        pt[a:a + CHUNK, at(t)] = p
        part = jnp.dot(rta[:, a:a + CHUNK], p, preferred_element_type=f32)
        return part if total is None else total + part

    def stage(ahead, s_ahead, t, s_now):
        best, total = None, None
        peak = None if t is None else m_ref[:, at(t)]
        for a in range(0, nr, CHUNK):
            if ahead is not None:
                best = score(ahead, s_ahead, a, best)
            if t is not None:
                total = weigh(t, s_now, a, peak, total)
        if ahead is not None:
            m_ref[:, at(ahead)] = best
        if t is not None:
            ut[:, at(t)] = total

    def all_to(src, dst, send, recv):
        def copy(k):
            return pltpu.make_async_remote_copy(
                src_ref=src, dst_ref=dst.at[k - 1], send_sem=send.at[k - 1], recv_sem=recv.at[k - 1],
                device_id={"ref": peer_of(k)}, device_id_type=pl.DeviceIdType.MESH,
            )

        def begin(k, carry):
            copy(k).start()
            return carry

        def end(k, carry):
            copy(k).wait()
            return carry

        return (lambda: lax.fori_loop(1, n, begin, 0)), (lambda: lax.fori_loop(1, n, end, 0))

    def spread_lse(g):
        cols = slice(g * half, (g + 1) * half)
        lse[g][...] = m_ref[:, cols] + jnp.log(ut[nf:nf + 1, cols]) * LOG2E
        all_to(lse[g], lse_rx[g], ls_send[g], ls_recv[g])[0]()

    def coefficients(g):
        cols = slice(g * half, (g + 1) * half)
        all_to(lse[g], lse_rx[g], ls_send[g], ls_recv[g])[1]()
        every = lse_rx[g][...]
        mine = lse[g][...]
        top = jnp.maximum(mine, jnp.max(every, axis=0))
        whole = jnp.exp2(mine - top) + jnp.sum(jnp.exp2(every - top[None]), axis=0)
        return cot_ref[:, cols] * jnp.exp2(m_ref[:, cols] - top) / whole

    def halving(g, i):
        size = 2 ** orders[g][i]
        bit = lax.rem(me // size, 2)
        return bit, pltpu.make_async_remote_copy(
            src_ref=acc[g][i].at[:, 1 - bit], dst_ref=got[g][i],
            send_sem=rs_send[g].at[i], recv_sem=rs_recv[g].at[i],
            device_id={"ref": me + (1 - 2 * bit) * size}, device_id_type=pl.DeviceIdType.MESH,
        )

    top_bit = lax.rem(me // (n // 2), 2)
    final = pltpu.make_async_remote_copy(
        src_ref=fin.at[1 - top_bit], dst_ref=fin_got, send_sem=fin_sem.at[0], recv_sem=fin_sem.at[1],
        device_id={"ref": me + (1 - 2 * top_bit) * (n // 2)}, device_id_type=pl.DeviceIdType.MESH,
    )

    def place_block(ref, shape, k, value):
        low = shape[2]
        ref[k // (2 * low), (k // low) % 2, k % low] = value

    def pull(g, coef):
        terms = jnp.zeros((1, nf), f32)
        for a in range(0, half, TILE):
            rows = slice(g * half + a, g * half + a + TILE)
            part = jnp.transpose(ut[0:nf, rows] * coef[:, a:a + TILE])
            terms = terms + jnp.sum(part * q_ref[rows, :], axis=0, keepdims=True)
            for b in range(0, TILE, own):
                place_block(acc[g][0], shapes[g][0], (a + b) // own, part[b:b + own])
        halving(g, 0)[1].start()
        return terms

    def settle(g, i):
        bit, copy = halving(g, i)
        copy.wait()
        high, _, low = shapes[g][i]
        for k in range(high * low):
            value = acc[g][i][k // low, bit, k % low] + got[g][i][k // low, k % low]
            if i + 1 < last:
                place_block(acc[g][i + 1], shapes[g][i + 1], k, value)
            else:
                fin[g] = value
        if i + 1 < last:
            halving(g, i + 1)[1].start()
        else:
            @pl.when(top_bit != g)
            def _():
                final.start()

    row = lax.broadcasted_iota(jnp.int32, (nf, TILE), 0)

    def scale_queries(g, coef):
        for a in range(0, half, TILE):
            rows = slice(g * half + a, g * half + a + TILE)
            c = coef[:, a:a + TILE]
            c1, c2, _ = split3(c)
            extra = jnp.where(row == 0, c1, jnp.where(row == 1, c2, 0.0))
            xt[rows, 0:nf] = jnp.transpose(qt[:, rows] * c).astype(bf16)
            xt[rows, nf:2 * nf] = jnp.transpose(extra).astype(bf16)

    def pushed(g, i):
        rows = slice(i * CHUNK, (i + 1) * CHUNK)
        cols = slice(g * half, (g + 1) * half)
        return jnp.dot(pt[rows, cols], xt[cols, :], preferred_element_type=f32)

    stores = [
        pltpu.make_async_copy(
            rg_ref.at[pl.ds(i * CHUNK, CHUNK)], rg_hbm.at[pl.ds(i * CHUNK, CHUNK)], rg_sem.at[i]
        )
        for i in range(nr // CHUNK)
    ]

    def finish(i, terms):
        rows = slice(i * CHUNK, (i + 1) * CHUNK)
        both = push[rows, :] + pushed(1, i)
        r = r_ref[rows, :]
        column = both[:, nf:nf + 1] + both[:, nf + 1:nf + 2]
        grad = (both[:, 0:nf] - r * column) * inv
        rg_ref[rows, :] = grad
        stores[i].start()
        return terms + jnp.sum(r * grad, axis=0, keepdims=True)

    tiles = nq // TILE
    chunks = nr // CHUNK
    stage(0, s0, None, None)

    def pair(t, carry):
        stage(2 * t + 1, s1, 2 * t, s0)
        stage(2 * t + 2, s0, 2 * t + 1, s1)
        return carry

    lax.fori_loop(0, tiles // 4, pair, 0)
    pl.semaphore_wait(barrier, n - 1)
    spread_lse(0)
    lax.fori_loop(tiles // 4, tiles // 2 - 1, pair, 0)
    coef = coefficients(0)
    terms = pull(0, coef)
    stage(tiles - 1, s1, tiles - 2, s0)
    settle(0, 0)
    stage(None, None, tiles - 1, s1)
    spread_lse(1)

    scale_queries(0, coef)
    for i in range(chunks):
        push[i * CHUNK:(i + 1) * CHUNK, :] = pushed(0, i)
    settle(0, 1)
    coef = coefficients(1)
    terms = (terms + pull(1, coef)) * inv
    scale_queries(1, coef)
    terms = finish(0, terms)
    settle(1, 0)
    for i in range(1, chunks):
        terms = finish(i, terms)
    term[...] = terms
    term_start, term_wait = all_to(term, term_rx, tm_send, tm_recv)
    term_start()
    for i in range(2, last):
        settle(0, i)
    for i in range(1, last):
        settle(1, i)
    cot_q = jnp.zeros((1, nf), f32)
    for a in range(0, nq, TILE):
        rows = slice(a, a + TILE)
        part = jnp.transpose(qt[:, rows] * cot_ref[:, rows])
        cq[rows, :] = part
        cot_q = cot_q + jnp.sum(part * q_ref[rows, :], axis=0, keepdims=True)
    for store in stores:
        store.wait()
    term_wait()
    summed = terms + jnp.sum(term_rx[...], axis=0) - cot_q * inv
    sg_ref[...] = -summed / sp - jnp.sum(cot_ref[...], axis=1, keepdims=True) / sp
    mine_rows = pl.ds(pl.multiple_of(me * own, own), own)
    final.wait()
    qg_ref[...] = (fin[top_bit] + fin_got[...] - cq[mine_rows, :]) * inv


def hand_out(*refs):
    sem = refs[-1]
    copies = [pltpu.make_async_copy(refs[i], refs[3 + i], sem.at[i]) for i in range(3)]
    for copy in copies:
        copy.start()
    for copy in copies:
        copy.wait()


def on_device(n, queries, references, query_ids, spread, cotangent):
    nq, nf = queries.shape
    nr = references.shape[0]
    own = nq // n
    half = nq // 2
    f32, bf16 = jnp.float32, jnp.bfloat16
    last, _ = plan(n)
    shapes = layouts(n)
    dma = pltpu.SemaphoreType.DMA
    scratch = [
        pltpu.VMEM((nr, nf), f32),
        dma((nr // CHUNK,)),
        pltpu.VMEM((1, nq), jnp.int32),
        pltpu.VMEM((1, nf), f32),
        pltpu.VMEM((1, nq), f32),
        dma((3,)),
        pltpu.VMEM((4 * nf, nq), bf16),
        pltpu.VMEM((nr, 4 * nf), bf16),
        pltpu.VMEM((nf + 16, nr), bf16),
        pltpu.VMEM((nr, nq), bf16),
        pltpu.VMEM((nr, TILE), f32),
        pltpu.VMEM((nr, TILE), f32),
        pltpu.VMEM((1, nq), f32),
        pltpu.VMEM((nf + 16, nq), f32),
        pltpu.VMEM((nq, nf), f32),
        pltpu.VMEM((nf, nq), f32),
        pltpu.VMEM((nq, 2 * nf), bf16),
        pltpu.VMEM((nr, 2 * nf), f32),
        pltpu.VMEM((2, own, nf), f32),
        pltpu.VMEM((own, nf), f32),
        pltpu.VMEM((1, nf), f32),
        pltpu.VMEM((n - 1, 1, nf), f32),
    ]
    scratch += [pltpu.VMEM((1, half), f32)] * 2
    scratch += [pltpu.VMEM((n - 1, 1, half), f32)] * 2
    scratch += [pltpu.VMEM(shape + (own, nf), f32) for group in shapes for shape in group]
    scratch += [pltpu.VMEM((h, l, own, nf), f32) for group in shapes for h, _, l in group]
    scratch += [dma((n - 1,))] * 4 + [dma((last,))] * 4 + [dma((n - 1,))] * 2 + [dma((2,))]
    vmem = pl.BlockSpec(memory_space=pltpu.VMEM)
    hbm = pl.BlockSpec(memory_space=pltpu.HBM)
    shapes_out = (
        jax.ShapeDtypeStruct((own, nf), f32),
        jax.ShapeDtypeStruct((nr, nf), f32),
        jax.ShapeDtypeStruct((1, nf), f32),
    )
    results = pl.pallas_call(
        functools.partial(kernel, n),
        out_shape=shapes_out,
        in_specs=[vmem, vmem, hbm, hbm, hbm],
        out_specs=(vmem, hbm, vmem),
        scratch_shapes=scratch,
        compiler_params=pltpu.CompilerParams(
            collective_id=0, has_side_effects=True, vmem_limit_bytes=62 * 2 ** 20
        ),
    )(queries, references, query_ids[None, :], spread[None, :], cotangent[None, :])
    query_grad, reference_grad, spread_grad = pl.pallas_call(
        hand_out,
        out_shape=shapes_out,
        in_specs=[pl.BlockSpec(memory_space=pl.ANY)] * 3,
        out_specs=(hbm, hbm, hbm),
        scratch_shapes=[dma((3,))],
        compiler_params=pltpu.CompilerParams(vmem_limit_bytes=62 * 2 ** 20),
    )(*results)
    return query_grad, reference_grad, spread_grad[0]


def solution(mesh):
    placed = (P("parts", None), P(("parts", "ref"), None), P("parts"), P(), P("parts"))
    return jax.shard_map(
        functools.partial(on_device, mesh.shape["ref"]),
        mesh=mesh,
        in_specs=placed,
        out_specs=(P(("parts", "ref"), None), P(("parts", "ref"), None), P("parts")),
        check_vma=False,
    )
```

time: 42.1 us -> 72.6 us (1.72)
  Pallas kernels: 37 us -> 71.8 us
  local copies, waits for them, and re-layouts: 4.15 us -> 0 us
    pallas_call x1 -> x2, Pallas kernels: 37 us -> 71.8 us  [the longest x1 36.9 us: on_device(): pl.pallas_call(functools.partial(kernel, n), out_shape=shapes_out, in_spe...]
    unnamed x9 -> x0, local copies, waits for them, and re-layouts: 4.15 us -> none
where the time goes in v2:
time: 72.6 us; the launch traced here: 72.4 us
  Pallas kernels  71.8 us (99%)
    pallas_call x1, Pallas kernels, on_device(): pl.pallas_call(functools.partial(kernel, n), out_shape=shapes_out, in_spe...  36.9 us
    pallas_call x1, Pallas kernels, on_device(): pl.pallas_call(hand_out, out_shape=shapes_out, in_specs=[pl.BlockSpec(mem...  34.9 us

profile of v2, /device:TPU:0, one launch (start us, length us, event | category | flops | bytes accessed | tf_op | source)
XLA Modules:
  0.0 72.4 jit_solution(5374351994822220636)
XLA Ops:
  0.6 36.9 %shard_map.76 = (f32[128,128]{1,0:T(8,128)}, f32[2048,128]{1,0:T(8,128)}, f32[1,128]{1,0:T(1,128)}) custom-call(f32[2048,128]{1,0:T(8,128)} %q_ref.1, f32[2048,128]{1,0:T(8,128)} %r_ref.1, s32[1,2048]{1,0:T(1,128)} %bitcast.4, f32[1,128]{1,0:T(1,128)} %bitcast.6, f32[1,2048]{1,0:T(1,128)} %bitcast.5), custom_call_target="tpu_custom_call" | custom-call | tf_op jit(solution)/shard_map/pallas_call | solution.py:381
  37.5 34.9 %shard_map.77 = (f32[128,128]{1,0:T(8,128)}, f32[2048,128]{1,0:T(8,128)}, f32[1,128]{1,0:T(1,128)}) custom-call(f32[128,128]{1,0:T(8,128)} %get-tuple-element.9.refs_0_, f32[2048,128]{1,0:T(8,128)} %get-tuple-element.10.refs_1_, f32[1,128]{1,0:T(1,128)} %get-tuple-element.11.refs_2_), custom_call_target="tpu_custom_call" | custom-call | tf_op jit(solution)/shard_map/pallas_call | solution.py:391

commit v3 on v2

--- a/solution.py
+++ b/solution.py
@@ -11,6 +11,7 @@
 LOG2E = math.log2(math.e)
 TILE = 256
 CHUNK = 512
+SPAN = 1024
 
 
 def split3(x):
@@ -45,7 +46,7 @@
 def kernel(
     n, q_ref, r_ref, ids_hbm, sp_hbm, cot_hbm, qg_ref, rg_hbm, sg_ref,
     rg_ref, rg_sem, ids_ref, sp_ref, cot_ref, in_sem,
-    qat, ra, rta, pt, s0, s1, m_ref, ut, cq, qt, xt, push, fin, fin_got, term, term_rx, *rest
+    qat, ra, rta, pt, s0, s1, m_ref, ut, qt, xt, push, fin, fin_got, term, term_rx, *rest
 ):
     last, orders = plan(n)
     shapes = layouts(n)
@@ -123,7 +124,7 @@
         ext = jnp.where(place == 4, n2, ext)
         ext = jnp.where(place == 5, n3, ext)
         ra[rows, 3 * nf:4 * nf] = ext.astype(bf16)
-        rta[0:nf, rows] = jnp.transpose(r).astype(bf16)
+        rta[0:nf, rows] = jnp.transpose(high)
     rta[nf:nf + 16, :] = jnp.ones((16, nr), bf16)
 
     start = me * nr
@@ -132,24 +133,24 @@
         return pl.ds(pl.multiple_of(t * TILE, TILE), TILE)
 
     def score(t, s_ref, a, best):
-        s = jnp.dot(ra[a:a + CHUNK, :], qat[:, at(t)], preferred_element_type=f32)
+        s = jnp.dot(ra[a:a + SPAN, :], qat[:, at(t)], preferred_element_type=f32)
         local = ids_ref[:, at(t)] - (start + a)
-        hit = lax.broadcasted_iota(jnp.int32, (CHUNK, TILE), 0) == local
+        hit = lax.broadcasted_iota(jnp.int32, (SPAN, TILE), 0) == local
         s = jnp.where(hit, -jnp.inf, s)
-        s_ref[a:a + CHUNK, :] = s
+        s_ref[a:a + SPAN, :] = s
         top = jnp.max(s, axis=0, keepdims=True)
         return top if best is None else jnp.maximum(best, top)
 
     def weigh(t, s_ref, a, peak, total):
-        p = jnp.exp2(s_ref[a:a + CHUNK, :] - peak).astype(bf16)
-        pt[a:a + CHUNK, at(t)] = p
-        part = jnp.dot(rta[:, a:a + CHUNK], p, preferred_element_type=f32)
+        p = jnp.exp2(s_ref[a:a + SPAN, :] - peak).astype(bf16)
+        pt[a:a + SPAN, at(t)] = p
+        part = jnp.dot(rta[:, a:a + SPAN], p, preferred_element_type=f32)
         return part if total is None else total + part
 
     def stage(ahead, s_ahead, t, s_now):
         best, total = None, None
         peak = None if t is None else m_ref[:, at(t)]
-        for a in range(0, nr, CHUNK):
+        for a in range(0, nr, SPAN):
             if ahead is not None:
                 best = score(ahead, s_ahead, a, best)
             if t is not None:
@@ -213,7 +214,9 @@
         terms = jnp.zeros((1, nf), f32)
         for a in range(0, half, TILE):
             rows = slice(g * half + a, g * half + a + TILE)
-            part = jnp.transpose(ut[0:nf, rows] * coef[:, a:a + TILE])
+            part = jnp.transpose(
+                ut[0:nf, rows] * coef[:, a:a + TILE] - qt[:, rows] * (cot_ref[:, rows] * (1.0 / n))
+            )
             terms = terms + jnp.sum(part * q_ref[rows, :], axis=0, keepdims=True)
             for b in range(0, TILE, own):
                 place_block(acc[g][0], shapes[g][0], (a + b) // own, part[b:b + own])
@@ -237,21 +240,20 @@
             def _():
                 final.start()
 
-    row = lax.broadcasted_iota(jnp.int32, (nf, TILE), 0)
+    row = lax.broadcasted_iota(jnp.int32, (16, half), 0)
 
     def scale_queries(g, coef):
-        for a in range(0, half, TILE):
-            rows = slice(g * half + a, g * half + a + TILE)
-            c = coef[:, a:a + TILE]
-            c1, c2, _ = split3(c)
-            extra = jnp.where(row == 0, c1, jnp.where(row == 1, c2, 0.0))
-            xt[rows, 0:nf] = jnp.transpose(qt[:, rows] * c).astype(bf16)
-            xt[rows, nf:2 * nf] = jnp.transpose(extra).astype(bf16)
+        cols = slice(g * half, (g + 1) * half)
+        c1, c2, _ = split3(coef)
+        xt[0:nf, cols] = (qt[:, cols] * coef).astype(bf16)
+        xt[nf:nf + 16, cols] = jnp.where(row == 0, c1, jnp.where(row == 1, c2, 0.0)).astype(bf16)
 
     def pushed(g, i):
         rows = slice(i * CHUNK, (i + 1) * CHUNK)
         cols = slice(g * half, (g + 1) * half)
-        return jnp.dot(pt[rows, cols], xt[cols, :], preferred_element_type=f32)
+        return lax.dot_general(
+            pt[rows, cols], xt[:, cols], (((1,), (1,)), ((), ())), preferred_element_type=f32
+        )
 
     stores = [
         pltpu.make_async_copy(
@@ -308,29 +310,30 @@
         settle(0, i)
     for i in range(1, last):
         settle(1, i)
-    cot_q = jnp.zeros((1, nf), f32)
-    for a in range(0, nq, TILE):
-        rows = slice(a, a + TILE)
-        part = jnp.transpose(qt[:, rows] * cot_ref[:, rows])
-        cq[rows, :] = part
-        cot_q = cot_q + jnp.sum(part * q_ref[rows, :], axis=0, keepdims=True)
     for store in stores:
         store.wait()
     term_wait()
-    summed = terms + jnp.sum(term_rx[...], axis=0) - cot_q * inv
+    summed = terms + jnp.sum(term_rx[...], axis=0)
     sg_ref[...] = -summed / sp - jnp.sum(cot_ref[...], axis=1, keepdims=True) / sp
-    mine_rows = pl.ds(pl.multiple_of(me * own, own), own)
     final.wait()
-    qg_ref[...] = (fin[top_bit] + fin_got[...] - cq[mine_rows, :]) * inv
-
-
-def hand_out(*refs):
-    sem = refs[-1]
-    copies = [pltpu.make_async_copy(refs[i], refs[3 + i], sem.at[i]) for i in range(3)]
-    for copy in copies:
-        copy.start()
-    for copy in copies:
-        copy.wait()
+    qg_ref[...] = (fin[top_bit] + fin_got[...]) * inv
+
+
+def hand_out(qg_in, rg_in, sg_in, qg_out, rg_out, sg_out, qg, rg, sg, load_sem, store_sem):
+    rows = rg.shape[0]
+    parts = [(qg_in, qg, qg_out), (sg_in, sg, sg_out)]
+    for a in range(0, rows, CHUNK):
+        piece = pl.ds(a, CHUNK)
+        parts.append((rg_in.at[piece], rg.at[piece], rg_out.at[piece]))
+    loads = [pltpu.make_async_copy(x, y, load_sem.at[i]) for i, (x, y, _) in enumerate(parts)]
+    stores = [pltpu.make_async_copy(y, z, store_sem.at[i]) for i, (_, y, z) in enumerate(parts)]
+    for load in loads:
+        load.start()
+    for load, store in zip(loads, stores):
+        load.wait()
+        store.start()
+    for store in stores:
+        store.wait()
 
 
 def on_device(n, queries, references, query_ids, spread, cotangent):
@@ -357,10 +360,9 @@
         pltpu.VMEM((nr, TILE), f32),
         pltpu.VMEM((1, nq), f32),
         pltpu.VMEM((nf + 16, nq), f32),
-        pltpu.VMEM((nq, nf), f32),
         pltpu.VMEM((nf, nq), f32),
-        pltpu.VMEM((nq, 2 * nf), bf16),
-        pltpu.VMEM((nr, 2 * nf), f32),
+        pltpu.VMEM((nf + 16, nq), bf16),
+        pltpu.VMEM((nr, nf + 16), f32),
         pltpu.VMEM((2, own, nf), f32),
         pltpu.VMEM((own, nf), f32),
         pltpu.VMEM((1, nf), f32),
@@ -393,7 +395,8 @@
         out_shape=shapes_out,
         in_specs=[pl.BlockSpec(memory_space=pl.ANY)] * 3,
         out_specs=(hbm, hbm, hbm),
-        scratch_shapes=[dma((3,))],
+        scratch_shapes=[pltpu.VMEM(x.shape, f32) for x in shapes_out]
+        + [dma((2 + nr // CHUNK,))] * 2,
         compiler_params=pltpu.CompilerParams(vmem_limit_bytes=62 * 2 ** 20),
     )(*results)
     return query_grad, reference_grad, spread_grad[0]

time: 72.6 us -> 39.6 us (0.55)
  Pallas kernels: 71.8 us -> 38.7 us
    pallas_call x1, Pallas kernels: 34.9 us -> 2.06 us  [on_device(): pl.pallas_call(hand_out, out_shape=shapes_out, in_specs=[pl.BlockSpec(mem...]
where the time goes in v3:
time: 39.6 us; the launch traced here: 39.3 us
  Pallas kernels  38.7 us (98%)
  between operations  0.64 us (2%)
    pallas_call x1, Pallas kernels, on_device(): pl.pallas_call(functools.partial(kernel, n), out_shape=shapes_out, in_spe...  36.6 us
    pallas_call x1, Pallas kernels, on_device(): pl.pallas_call(hand_out, out_shape=shapes_out, in_specs=[pl.BlockSpec(mem...  2.06 us

profile of v3, /device:TPU:0, one launch (start us, length us, event | category | flops | bytes accessed | tf_op | source)
XLA Modules:
  0.0 39.3 jit_solution(6530173361690630220)
XLA Ops:
  0.6 36.6 %shard_map.76 = (f32[128,128]{1,0:T(8,128)}, f32[2048,128]{1,0:T(8,128)}, f32[1,128]{1,0:T(1,128)}) custom-call(f32[2048,128]{1,0:T(8,128)} %q_ref.1, f32[2048,128]{1,0:T(8,128)} %r_ref.1, s32[1,2048]{1,0:T(1,128)} %bitcast.4, f32[1,128]{1,0:T(1,128)} %bitcast.6, f32[1,2048]{1,0:T(1,128)} %bitcast.5), custom_call_target="tpu_custom_call" | custom-call | tf_op jit(solution)/shard_map/pallas_call | solution.py:383
  37.3 2.1 %shard_map.77 = (f32[128,128]{1,0:T(8,128)}, f32[2048,128]{1,0:T(8,128)}, f32[1,128]{1,0:T(1,128)}) custom-call(f32[128,128]{1,0:T(8,128)} %get-tuple-element.9.qg_in, f32[2048,128]{1,0:T(8,128)} %get-tuple-element.10.rg_in, f32[1,128]{1,0:T(1,128)} %get-tuple-element.11.sg_in), custom_call_target="tpu_custom_call" | custom-call | tf_op jit(solution)/shard_map/pallas_call | solution.py:393

commit v4 on v3

--- a/solution.py
+++ b/solution.py
@@ -21,12 +21,13 @@
     return a, b, c
 
 
+GROUPS = 4
+TURN = (0, 3, 1, 2)
+
+
 def plan(n):
-    last = n.bit_length() - 2
-    mid = (last + 1) // 2
-    first = list(range(last))
-    second = [0] + [b for b in range(mid, last)] + [b for b in range(1, mid)]
-    return last, (first, second)
+    last = n.bit_length() - 3
+    return last, [list(range(last))] * GROUPS
 
 
 def layouts(n):
@@ -51,17 +52,16 @@
     last, orders = plan(n)
     shapes = layouts(n)
     rest = list(rest)
-    lse = [rest.pop(0) for _ in range(2)]
-    lse_rx = [rest.pop(0) for _ in range(2)]
-    acc = [[rest.pop(0) for _ in range(last)] for _ in range(2)]
-    got = [[rest.pop(0) for _ in range(last)] for _ in range(2)]
-    ls_send, ls_recv = rest[0:2], rest[2:4]
-    rs_send, rs_recv = rest[4:6], rest[6:8]
-    tm_send, tm_recv, fin_sem = rest[8:]
+    lse = [rest.pop(0) for _ in range(GROUPS)]
+    lse_rx = [rest.pop(0) for _ in range(GROUPS)]
+    acc = [[rest.pop(0) for _ in range(last)] for _ in range(GROUPS)]
+    got = [[rest.pop(0) for _ in range(last)] for _ in range(GROUPS)]
+    ls_send, ls_recv, rs_send, rs_recv = (rest[i * GROUPS:(i + 1) * GROUPS] for i in range(4))
+    tm_send, tm_recv, fin_send, fin_recv = rest[4 * GROUPS:]
     nq, nf = q_ref.shape
     nr = r_ref.shape[0]
     own = nq // n
-    half = nq // 2
+    half = nq // GROUPS
     f32, bf16 = jnp.float32, jnp.bfloat16
     me = lax.axis_index("ref")
 
@@ -200,11 +200,16 @@
             device_id={"ref": me + (1 - 2 * bit) * size}, device_id_type=pl.DeviceIdType.MESH,
         )
 
-    top_bit = lax.rem(me // (n // 2), 2)
-    final = pltpu.make_async_remote_copy(
-        src_ref=fin.at[1 - top_bit], dst_ref=fin_got, send_sem=fin_sem.at[0], recv_sem=fin_sem.at[1],
-        device_id={"ref": me + (1 - 2 * top_bit) * (n // 2)}, device_id_type=pl.DeviceIdType.MESH,
-    )
+    far = n // GROUPS
+    group = lax.rem(me // far, GROUPS)
+
+    def final(j):
+        to = lax.rem(group + j, GROUPS)
+        return pltpu.make_async_remote_copy(
+            src_ref=fin.at[to], dst_ref=fin_got.at[j - 1],
+            send_sem=fin_send.at[j - 1], recv_sem=fin_recv.at[j - 1],
+            device_id={"ref": me + (to - group) * far}, device_id_type=pl.DeviceIdType.MESH,
+        )
 
     def place_block(ref, shape, k, value):
         low = shape[2]
@@ -236,9 +241,8 @@
         if i + 1 < last:
             halving(g, i + 1)[1].start()
         else:
-            @pl.when(top_bit != g)
-            def _():
-                final.start()
+            for j in range(1, GROUPS):
+                pl.when(group == (g - j) % GROUPS)(final(j).start)
 
     row = lax.broadcasted_iota(jnp.int32, (16, half), 0)
 
@@ -248,9 +252,9 @@
         xt[0:nf, cols] = (qt[:, cols] * coef).astype(bf16)
         xt[nf:nf + 16, cols] = jnp.where(row == 0, c1, jnp.where(row == 1, c2, 0.0)).astype(bf16)
 
-    def pushed(g, i):
+    def pushed(g, end, i):
         rows = slice(i * CHUNK, (i + 1) * CHUNK)
-        cols = slice(g * half, (g + 1) * half)
+        cols = slice(g * half, end * half)
         return lax.dot_general(
             pt[rows, cols], xt[:, cols], (((1,), (1,)), ((), ())), preferred_element_type=f32
         )
@@ -264,7 +268,7 @@
 
     def finish(i, terms):
         rows = slice(i * CHUNK, (i + 1) * CHUNK)
-        both = push[rows, :] + pushed(1, i)
+        both = push[rows, :] + pushed(TURN[3], TURN[3] + 1, i)
         r = r_ref[rows, :]
         column = both[:, nf:nf + 1] + both[:, nf + 1:nf + 2]
         grad = (both[:, 0:nf] - r * column) * inv
@@ -272,51 +276,64 @@
         stores[i].start()
         return terms + jnp.sum(r * grad, axis=0, keepdims=True)
 
-    tiles = nq // TILE
+    per = half // TILE
+    order = [g * per + i for g in TURN for i in range(per)]
     chunks = nr // CHUNK
-    stage(0, s0, None, None)
-
-    def pair(t, carry):
-        stage(2 * t + 1, s1, 2 * t, s0)
-        stage(2 * t + 2, s0, 2 * t + 1, s1)
-        return carry
-
-    lax.fori_loop(0, tiles // 4, pair, 0)
-    pl.semaphore_wait(barrier, n - 1)
-    spread_lse(0)
-    lax.fori_loop(tiles // 4, tiles // 2 - 1, pair, 0)
-    coef = coefficients(0)
-    terms = pull(0, coef)
-    stage(tiles - 1, s1, tiles - 2, s0)
-    settle(0, 0)
-    stage(None, None, tiles - 1, s1)
-    spread_lse(1)
-
-    scale_queries(0, coef)
+    coefs = {}
+    terms = jnp.zeros((1, nf), f32)
+
+    def collect(g):
+        coefs[g] = coefficients(g)
+        return pull(g, coefs[g])
+
+    bufs = (s0, s1)
+    stage(order[0], s0, None, None)
+    for i, t in enumerate(order):
+        ahead = order[i + 1] if i + 1 < len(order) else None
+        stage(ahead, bufs[(i + 1) % 2], t, bufs[i % 2])
+        if (i + 1) % per:
+            continue
+        turn = (i + 1) // per - 1
+        if turn == 0:
+            pl.semaphore_wait(barrier, n - 1)
+        spread_lse(TURN[turn])
+        if turn >= 2:
+            settle(TURN[turn - 2], 0)
+        if turn >= 1:
+            terms = terms + collect(TURN[turn - 1])
+        if turn >= 2:
+            for k in range(1, last):
+                settle(TURN[turn - 2], k)
+
+    early = TURN[:3]
+    for g in early:
+        scale_queries(g, coefs[g])
     for i in range(chunks):
-        push[i * CHUNK:(i + 1) * CHUNK, :] = pushed(0, i)
-    settle(0, 1)
-    coef = coefficients(1)
-    terms = (terms + pull(1, coef)) * inv
-    scale_queries(1, coef)
-    terms = finish(0, terms)
-    settle(1, 0)
-    for i in range(1, chunks):
+        rows = slice(i * CHUNK, (i + 1) * CHUNK)
+        push[rows, :] = pushed(0, 2, i) + pushed(3, 4, i)
+        if i == 0:
+            settle(early[2], 0)
+    terms = (terms + collect(TURN[3])) * inv
+    scale_queries(TURN[3], coefs[TURN[3]])
+    for k in range(1, last):
+        settle(early[2], k)
+    for i in range(chunks):
         terms = finish(i, terms)
+        if i == chunks // 2 - 1:
+            settle(TURN[3], 0)
     term[...] = terms
     term_start, term_wait = all_to(term, term_rx, tm_send, tm_recv)
     term_start()
-    for i in range(2, last):
-        settle(0, i)
-    for i in range(1, last):
-        settle(1, i)
+    for k in range(1, last):
+        settle(TURN[3], k)
     for store in stores:
         store.wait()
     term_wait()
     summed = terms + jnp.sum(term_rx[...], axis=0)
     sg_ref[...] = -summed / sp - jnp.sum(cot_ref[...], axis=1, keepdims=True) / sp
-    final.wait()
-    qg_ref[...] = (fin[top_bit] + fin_got[...]) * inv
+    for j in range(1, GROUPS):
+        final(j).wait()
+    qg_ref[...] = (fin[group] + jnp.sum(fin_got[...], axis=0)) * inv
 
 
 def hand_out(qg_in, rg_in, sg_in, qg_out, rg_out, sg_out, qg, rg, sg, load_sem, store_sem):
@@ -340,7 +357,7 @@
     nq, nf = queries.shape
     nr = references.shape[0]
     own = nq // n
-    half = nq // 2
+    half = nq // GROUPS
     f32, bf16 = jnp.float32, jnp.bfloat16
     last, _ = plan(n)
     shapes = layouts(n)
@@ -363,16 +380,17 @@
         pltpu.VMEM((nf, nq), f32),
         pltpu.VMEM((nf + 16, nq), bf16),
         pltpu.VMEM((nr, nf + 16), f32),
-        pltpu.VMEM((2, own, nf), f32),
-        pltpu.VMEM((own, nf), f32),
+        pltpu.VMEM((GROUPS, own, nf), f32),
+        pltpu.VMEM((GROUPS - 1, own, nf), f32),
         pltpu.VMEM((1, nf), f32),
         pltpu.VMEM((n - 1, 1, nf), f32),
     ]
-    scratch += [pltpu.VMEM((1, half), f32)] * 2
-    scratch += [pltpu.VMEM((n - 1, 1, half), f32)] * 2
+    scratch += [pltpu.VMEM((1, half), f32)] * GROUPS
+    scratch += [pltpu.VMEM((n - 1, 1, half), f32)] * GROUPS
     scratch += [pltpu.VMEM(shape + (own, nf), f32) for group in shapes for shape in group]
     scratch += [pltpu.VMEM((h, l, own, nf), f32) for group in shapes for h, _, l in group]
-    scratch += [dma((n - 1,))] * 4 + [dma((last,))] * 4 + [dma((n - 1,))] * 2 + [dma((2,))]
+    scratch += [dma((n - 1,))] * (2 * GROUPS) + [dma((last,))] * (2 * GROUPS)
+    scratch += [dma((n - 1,))] * 2 + [dma((GROUPS - 1,))] * 2
     vmem = pl.BlockSpec(memory_space=pltpu.VMEM)
     hbm = pl.BlockSpec(memory_space=pltpu.HBM)
     shapes_out = (

time: 39.6 us -> 39.1 us (0.987)
  Pallas kernels: 38.7 us -> 38.2 us
    pallas_call x1, Pallas kernels: 36.6 us -> 36.2 us  [on_device(): pl.pallas_call(functools.partial(kernel, n), out_shape=shapes_out, in_spe...]
where the time goes in v4:
time: 39.1 us; the launch traced here: 38.9 us
  Pallas kernels  38.2 us (98%)
  between operations  0.64 us (2%)
    pallas_call x1, Pallas kernels, on_device(): pl.pallas_call(functools.partial(kernel, n), out_shape=shapes_out, in_spe...  36.2 us
    pallas_call x1, Pallas kernels, on_device(): pl.pallas_call(hand_out, out_shape=shapes_out, in_specs=[pl.BlockSpec(mem...  2.06 us

profile of v4, /device:TPU:0, one launch (start us, length us, event | category | flops | bytes accessed | tf_op | source)
XLA Modules:
  0.0 38.9 jit_solution(3834793969097123058)
XLA Ops:
  0.6 36.2 %shard_map.76 = (f32[128,128]{1,0:T(8,128)}, f32[2048,128]{1,0:T(8,128)}, f32[1,128]{1,0:T(1,128)}) custom-call(f32[2048,128]{1,0:T(8,128)} %q_ref.1, f32[2048,128]{1,0:T(8,128)} %r_ref.1, s32[1,2048]{1,0:T(1,128)} %bitcast.4, f32[1,128]{1,0:T(1,128)} %bitcast.6, f32[1,2048]{1,0:T(1,128)} %bitcast.5), custom_call_target="tpu_custom_call" | custom-call | tf_op jit(solution)/shard_map/pallas_call | solution.py:401
  36.8 2.1 %shard_map.77 = (f32[128,128]{1,0:T(8,128)}, f32[2048,128]{1,0:T(8,128)}, f32[1,128]{1,0:T(1,128)}) custom-call(f32[128,128]{1,0:T(8,128)} %get-tuple-element.9.qg_in, f32[2048,128]{1,0:T(8,128)} %get-tuple-element.10.rg_in, f32[1,128]{1,0:T(1,128)} %get-tuple-element.11.sg_in), custom_call_target="tpu_custom_call" | custom-call | tf_op jit(solution)/shard_map/pallas_call | solution.py:411

commit v5 on v4

--- a/solution.py
+++ b/solution.py
@@ -9,7 +9,7 @@
 from jax.sharding import PartitionSpec as P
 
 LOG2E = math.log2(math.e)
-TILE = 256
+TILE = 512
 CHUNK = 512
 SPAN = 1024
 
@@ -163,7 +163,7 @@
     def all_to(src, dst, send, recv):
         def copy(k):
             return pltpu.make_async_remote_copy(
-                src_ref=src, dst_ref=dst.at[k - 1], send_sem=send.at[k - 1], recv_sem=recv.at[k - 1],
+                src_ref=src, dst_ref=dst.at[k - 1], send_sem=send.at[0], recv_sem=recv.at[0],
                 device_id={"ref": peer_of(k)}, device_id_type=pl.DeviceIdType.MESH,
             )
 
@@ -171,11 +171,11 @@
             copy(k).start()
             return carry
 
-        def end(k, carry):
-            copy(k).wait()
-            return carry
-
-        return (lambda: lax.fori_loop(1, n, begin, 0)), (lambda: lax.fori_loop(1, n, end, 0))
+        def end():
+            pltpu.make_async_copy(dst, dst, send.at[0]).wait()
+            pltpu.make_async_copy(dst, dst, recv.at[0]).wait()
+
+        return (lambda: lax.fori_loop(1, n, begin, 0)), end
 
     def spread_lse(g):
         cols = slice(g * half, (g + 1) * half)
@@ -389,8 +389,8 @@
     scratch += [pltpu.VMEM((n - 1, 1, half), f32)] * GROUPS
     scratch += [pltpu.VMEM(shape + (own, nf), f32) for group in shapes for shape in group]
     scratch += [pltpu.VMEM((h, l, own, nf), f32) for group in shapes for h, _, l in group]
-    scratch += [dma((n - 1,))] * (2 * GROUPS) + [dma((last,))] * (2 * GROUPS)
-    scratch += [dma((n - 1,))] * 2 + [dma((GROUPS - 1,))] * 2
+    scratch += [dma((1,))] * (2 * GROUPS) + [dma((last,))] * (2 * GROUPS)
+    scratch += [dma((1,))] * 2 + [dma((GROUPS - 1,))] * 2
     vmem = pl.BlockSpec(memory_space=pltpu.VMEM)
     hbm = pl.BlockSpec(memory_space=pltpu.HBM)
     shapes_out = (

time: 39.1 us -> 38.1 us (0.974)
  Pallas kernels: 38.2 us -> 37.2 us
    pallas_call x1, Pallas kernels: 36.2 us -> 35.1 us  [on_device(): pl.pallas_call(functools.partial(kernel, n), out_shape=shapes_out, in_spe...]
where the time goes in v5:
time: 38.1 us; the launch traced here: 37.8 us
  Pallas kernels  37.2 us (98%)
  between operations  0.64 us (2%)
    pallas_call x1, Pallas kernels, on_device(): pl.pallas_call(functools.partial(kernel, n), out_shape=shapes_out, in_spe...  35.1 us
    pallas_call x1, Pallas kernels, on_device(): pl.pallas_call(hand_out, out_shape=shapes_out, in_specs=[pl.BlockSpec(mem...  2.06 us

profile of v5, /device:TPU:0, one launch (start us, length us, event | category | flops | bytes accessed | tf_op | source)
XLA Modules:
  0.0 37.8 jit_solution(6660527608664877582)
XLA Ops:
  0.6 35.1 %shard_map.76 = (f32[128,128]{1,0:T(8,128)}, f32[2048,128]{1,0:T(8,128)}, f32[1,128]{1,0:T(1,128)}) custom-call(f32[2048,128]{1,0:T(8,128)} %q_ref.1, f32[2048,128]{1,0:T(8,128)} %r_ref.1, s32[1,2048]{1,0:T(1,128)} %bitcast.4, f32[1,128]{1,0:T(1,128)} %bitcast.6, f32[1,2048]{1,0:T(1,128)} %bitcast.5), custom_call_target="tpu_custom_call" | custom-call | tf_op jit(solution)/shard_map/pallas_call | solution.py:401
  35.8 2.1 %shard_map.77 = (f32[128,128]{1,0:T(8,128)}, f32[2048,128]{1,0:T(8,128)}, f32[1,128]{1,0:T(1,128)}) custom-call(f32[128,128]{1,0:T(8,128)} %get-tuple-element.9.qg_in, f32[2048,128]{1,0:T(8,128)} %get-tuple-element.10.rg_in, f32[1,128]{1,0:T(1,128)} %get-tuple-element.11.sg_in), custom_call_target="tpu_custom_call" | custom-call | tf_op jit(solution)/shard_map/pallas_call | solution.py:411

commit v6 on v5

--- a/solution.py
+++ b/solution.py
@@ -90,8 +90,8 @@
     sp = sp_ref[...]
     inv = 1.0 / (sp * sp)
     inv_col = jnp.transpose(jnp.broadcast_to(inv, (8, nf)))[:, :1]
-    for a in range(0, nq, TILE):
-        rows = slice(a, a + TILE)
+    def prepare(t):
+        rows = slice(t * TILE, (t + 1) * TILE)
         q_t = jnp.transpose(q_ref[rows, :])
         qt[:, rows] = q_t
         scaled = q_t * (inv_col * LOG2E)
@@ -287,9 +287,13 @@
         return pull(g, coefs[g])
 
     bufs = (s0, s1)
+    prepare(order[0])
     stage(order[0], s0, None, None)
+    prepare(order[1])
     for i, t in enumerate(order):
         ahead = order[i + 1] if i + 1 < len(order) else None
+        if i + 2 < len(order):
+            prepare(order[i + 2])
         stage(ahead, bufs[(i + 1) % 2], t, bufs[i % 2])
         if (i + 1) % per:
             continue

time: 38.1 us -> 38 us (level)
  no operation moved by 1% of the time
where the time goes in v6:
time: 38 us; the launch traced here: 37.8 us
  Pallas kernels  37.1 us (98%)
  between operations  0.64 us (2%)
    pallas_call x1, Pallas kernels, on_device(): pl.pallas_call(functools.partial(kernel, n), out_shape=shapes_out, in_spe...  35.1 us
    pallas_call x1, Pallas kernels, on_device(): pl.pallas_call(hand_out, out_shape=shapes_out, in_specs=[pl.BlockSpec(mem...  2.06 us

profile of v6, /device:TPU:0, one launch (start us, length us, event | category | flops | bytes accessed | tf_op | source)
XLA Modules:
  0.0 37.8 jit_solution(10764455576370127754)
XLA Ops:
  0.6 35.1 %shard_map.76 = (f32[128,128]{1,0:T(8,128)}, f32[2048,128]{1,0:T(8,128)}, f32[1,128]{1,0:T(1,128)}) custom-call(f32[2048,128]{1,0:T(8,128)} %q_ref.1, f32[2048,128]{1,0:T(8,128)} %r_ref.1, s32[1,2048]{1,0:T(1,128)} %bitcast.4, f32[1,128]{1,0:T(1,128)} %bitcast.6, f32[1,2048]{1,0:T(1,128)} %bitcast.5), custom_call_target="tpu_custom_call" | custom-call | tf_op jit(solution)/shard_map/pallas_call | solution.py:405
  35.7 2.1 %shard_map.77 = (f32[128,128]{1,0:T(8,128)}, f32[2048,128]{1,0:T(8,128)}, f32[1,128]{1,0:T(1,128)}) custom-call(f32[128,128]{1,0:T(8,128)} %get-tuple-element.9.qg_in, f32[2048,128]{1,0:T(8,128)} %get-tuple-element.10.rg_in, f32[1,128]{1,0:T(1,128)} %get-tuple-element.11.sg_in), custom_call_target="tpu_custom_call" | custom-call | tf_op jit(solution)/shard_map/pallas_call | solution.py:415
